TPU v7x, 1024 devices: a whole 4x8x16 slice. The times are simulated.
1024 devices in a mesh: row: 64 (over z, y_lo, core), col: 16 (over y_hi, x).
Axes of the slice: x: 4, y: 8 (y_hi: 4, y_lo: 2; y = y_hi * 2 + y_lo), z: 16, core: 2. Of those that a mesh axis runs over, the one named last changes fastest.
Arguments:
- a_vals: bfloat16 [64, 128, 192, 192], P('row', 'col'), may hold values from -0.75 to 0.75
- a_rows: int32 [64, 128], P('row', 'col'), may hold values from 0 to 31, as said below
- a_cols: int32 [64, 128], P('row', 'col'), may hold values from 28 to 67, as said below
- a_count: int32 [64, 16], P('row', 'col'), may hold values from 1 to 8, as said below
- p_vals: bfloat16 [2048, 2, 192, 192], P(('row', 'col')), may hold values from -0.4375 to 0.4375
- p_cols: int32 [2048, 2], replicated, may hold values from 0 to 1, as said below
Outputs:
- galerkin: float32 [24576, 1344], P(('row', 'col'))
Inputs may be any that keep to these rules, and one draw needn't show every extreme that they name: `a_count`: live blocks of each tile; at least one tile has 8. `a_rows`: slot s of a group lies in the 32 // 16 block rows of tile s // 8, from (s // 8) * (32 // 16) on. a_cols - 32 - a_rows lies between -4 and 4. The two entries of p_cols[i], in either order, are c = (i % 32) // 16 and a coarse block that differs from c by one.
All inputs are finite; a program needn't handle non-finite values.
Results may differ from a plain program's by a relative error of at most 0.0029.
Values may be sent and summed in bfloat16 or wider, within the bound.
A program may use at most 32 MiB of HBM per device.

v0:
```python
import jax
import jax.numpy as jnp
from jax import lax
from jax.sharding import PartitionSpec as P

KP = 2
HB = 4
BAND = 7
RB = 32
CR = 2


HIGHEST = lax.Precision.HIGHEST


def from_behind(value, axis, by):
    count = lax.axis_size(axis)
    pairs = [(i, i + by) for i in range(count) if 0 <= i + by < count]
    return lax.ppermute(value, axis, pairs)


def slot_triple(blocks, left_rows, right_rows):
    product = jnp.einsum(
        "sxy,skyz->skxz", blocks, right_rows, preferred_element_type=jnp.float32
    ).astype(jnp.bfloat16)
    return jnp.einsum("suxw,stxz->sutwz", left_rows, product, preferred_element_type=jnp.float32)


def local(a_vals, a_rows, a_cols, a_count, p_vals, p_cols):
    block_size = a_vals.shape[-1]
    shard_rows = p_vals.shape[0]
    columns = lax.axis_size("col")
    per_aggregate = columns // CR
    row_index = lax.axis_index("row")
    col_index = lax.axis_index("col")
    reach = -(-HB // shard_rows)

    def neighbour(distance):
        return from_behind(p_vals, ("row", "col"), distance)

    before = [neighbour(distance) for distance in range(reach, 0, -1)]
    after = [neighbour(-distance) for distance in range(1, reach + 1)]
    extended = jnp.concatenate(before + [p_vals] + after, axis=0)
    blocks = a_vals[0]
    left_ids = a_rows[0]
    right_ids = a_cols[0]
    live_count = a_count[0, 0]
    first_row = col_index * shard_rows
    left_rows = p_vals[left_ids - first_row]
    right_rows = extended[right_ids - RB - first_row + reach * shard_rows]
    left_global = row_index * RB + left_ids
    right_global = jnp.clip((row_index - 1) * RB + right_ids, 0, p_cols.shape[0] - 1)
    left_coarse = p_cols[left_global]
    tile_aggregate = col_index // per_aggregate
    window_row = left_coarse - tile_aggregate + 1
    right_coarse = (right_ids // RB - 1)[:, None] * CR + p_cols[right_global]
    offset = right_coarse[:, None, :] - left_coarse[:, :, None] + BAND // 2
    slot_count = blocks.shape[0]
    slot_live = (jnp.arange(slot_count, dtype=jnp.int32) < live_count).astype(jnp.float32)
    row_hot = (window_row[..., None] == jnp.arange(3, dtype=jnp.int32)).astype(jnp.float32)
    row_hot = row_hot * slot_live[:, None, None]
    offset_hot = (offset[..., None] == jnp.arange(BAND, dtype=jnp.int32)).astype(jnp.float32)
    weights = jnp.einsum("sue,sutd->suted", row_hot, offset_hot)
    weights = weights.reshape(slot_count, KP, KP, 3 * BAND)
    triple = slot_triple(blocks, left_rows, right_rows)
    gathered = jnp.einsum("sutq,sutwz->qwz", weights, triple, precision=HIGHEST)
    window = jnp.transpose(gathered.reshape(3, BAND, block_size, block_size), (0, 2, 1, 3))
    flat = window.reshape(3, block_size, BAND * block_size)
    holder = jnp.zeros((CR + 2, block_size, BAND * block_size), jnp.float32)
    holder = lax.dynamic_update_slice(holder, flat, (tile_aggregate, jnp.int32(0), jnp.int32(0)))
    full = holder[1 : CR + 1].reshape(CR * block_size, BAND * block_size)
    return lax.psum_scatter(full, "col", scatter_dimension=0, tiled=True)


def solution(mesh):
    placed = (
        P("row", "col", None, None),
        P("row", "col"),
        P("row", "col"),
        P("row", "col"),
        P(("row", "col"), None, None, None),
        P(),
    )
    return jax.shard_map(
        local, mesh=mesh, in_specs=placed, out_specs=P(("row", "col"), None), check_vma=False
    )
```

profile of v0, /device:TPU:1, one launch (start us, length us, event | category | flops | bytes accessed | tf_op | source)
XLA Modules:
  0.0 214.9 jit_solution(5111816962742009902)
XLA Ops:
  6.5 9.9 %collective-permute-start.3 = (bf16[2,2,192,192]{3,2,1,0:T(8,128)(2,1)}, bf16[2,2,192,192]{3,2,1,0:T(8,128)(2,1)S(1)}, u32[]{:S(2)}, u32[]{:S(2)}) collective-permute-start(bf16[2,2,192,192]{3,2,1,0:T(8,128)(2,1)} %param.10), channel_id=1, source_target_pairs={{2,0},{3,1},{4,2},{5,3},{6,4},{7,5},{8,6},{9,7},{10,8},{11,9},{12,... | collective-permute-start | bytes 884744 | tf_op jit(solution)/shard_map/ppermute | solution.py:19
  16.4 3.0 %collective-permute-start.2 = (bf16[2,2,192,192]{3,2,1,0:T(8,128)(2,1)}, bf16[2,2,192,192]{3,2,1,0:T(8,128)(2,1)S(1)}, u32[]{:S(2)}, u32[]{:S(2)}) collective-permute-start(bf16[2,2,192,192]{3,2,1,0:T(8,128)(2,1)} %param.10), channel_id=1, source_target_pairs={{1,0},{2,1},{3,2},{4,3},{5,4},{6,5},{7,6},{8,7},{9,8},{10,9},{11,1... | collective-permute-start | bytes 884744 | tf_op jit(solution)/shard_map/ppermute | solution.py:19
  19.5 2.2 %collective-permute-start.1 = (bf16[2,2,192,192]{3,2,1,0:T(8,128)(2,1)}, bf16[2,2,192,192]{3,2,1,0:T(8,128)(2,1)}, u32[]{:S(2)}, u32[]{:S(2)}) collective-permute-start(bf16[2,2,192,192]{3,2,1,0:T(8,128)(2,1)} %param.10), channel_id=1, source_target_pairs={{0,1},{1,2},{2,3},{3,4},{4,5},{5,6},{6,7},{7,8},{8,9},{9,10},{10,1... | collective-permute-start | bytes 884744 | tf_op jit(solution)/shard_map/ppermute | solution.py:19
  21.7 2.6 %collective-permute-start = (bf16[2,2,192,192]{3,2,1,0:T(8,128)(2,1)}, bf16[2,2,192,192]{3,2,1,0:T(8,128)(2,1)}, u32[]{:S(2)}, u32[]{:S(2)}) collective-permute-start(bf16[2,2,192,192]{3,2,1,0:T(8,128)(2,1)} %param.10), channel_id=1, source_target_pairs={{0,2},{1,3},{2,4},{3,5},{4,6},{5,7},{6,8},{7,9},{8,10},{9,11},{10,... | collective-permute-start | bytes 884744 | tf_op jit(solution)/shard_map/ppermute | solution.py:19
  24.9 0.7 add_multiply_fusion
  25.6 0.7 fusion.12
  26.3 1.1 copy.16
  27.4 0.6 gather_fusion.1
  29.2 0.7 reshape.211
  29.9 0.6 gather_fusion.3
  30.6 16.3 %collective-permute-done = bf16[2,2,192,192]{3,2,1,0:T(8,128)(2,1)} collective-permute-done((bf16[2,2,192,192]{3,2,1,0:T(8,128)(2,1)}, bf16[2,2,192,192]{3,2,1,0:T(8,128)(2,1)}, u32[]{:S(2)}, u32[]{:S(2)}) %collective-permute-start) | collective-permute-done | bytes 294944 | tf_op jit(solution)/shard_map/ppermute | solution.py:19
  46.9 1.8 constant_dynamic-update-slice_fusion.4
  48.6 1.8 constant_dynamic-update-slice_fusion.3
  50.4 0.8 constant_dynamic-update-slice_fusion.2
  51.2 0.8 constant_dynamic-update-slice_fusion.1
  52.0 0.8 constant_dynamic-update-slice_fusion
  52.8 3.3 %gather_fusion.2 = bf16[8,2,192,192]{3,2,1,0:T(8,128)(2,1)} fusion(bf16[10,2,192,192]{3,2,1,0:T(8,128)(2,1)} %constant_dynamic-update-slice_fusion, s32[1024]{0:T(1024)S(1)} %pad_clamp_fusion.1), kind=kCustom, calls=%fused_computation.2 | custom fusion | bytes 2359328 | tf_op jit(solution)/shard_map/gather | solution.py:50
  56.1 5.7 %convolution_bitcast_fusion = f32[8,2,2,192,192]{3,4,1,2,0:T(8,128)} fusion(bf16[8,2,192,192]{3,2,1,0:T(8,128)(2,1)S(1)} %gather_fusion.3, bf16[8,2,192,192]{3,2,1,0:T(8,128)(2,1)} %gather_fusion.2, bf16[1,8,192,192]{3,2,1,0:T(8,128)(2,1)S(1)} %copy-done), kind=kOutput, calls=%fused_computation.6 | convolution fusion | flops 680067072 | bytes 7667712 | tf_op jit(solution)/shard_map/suxw,stxz->sutwz/dot_general | solution.py:26
  61.8 7.3 %copy.24 = f32[8,2,2,192,192]{4,0,1,2,3:T(8,128)} copy(f32[8,2,2,192,192]{3,4,1,2,0:T(8,128)} %convolution_bitcast_fusion) | data formatting | bytes 9437184 | tf_op jit(solution)/shard_map/suxw,stxz->sutwz/transpose | solution.py:26
  69.1 8.0 %fusion.2 = f32[3,192,7,192]{3,2,1,0:T(8,128)} fusion(f32[8,2,2,192,192]{4,0,1,2,3:T(8,128)} %copy.24, f32[3,7,8,2,2,1]{1,0,2,3,4,5:T(4,128)S(1)} %bitcast.76), kind=kOutput, calls=%fused_computation.7 | convolution fusion | flops 297271296 | bytes 7817856 | tf_op jit(solution)/shard_map/sutq,sutwz->qwz/dot_general | solution.py:66
  77.1 5.0 %reshape.171 = f32[3,192,1344]{2,1,0:T(8,128)} reshape(f32[3,192,7,192]{3,2,1,0:T(8,128)} %fusion.2) | data formatting | bytes 6193152 | tf_op jit(solution)/shard_map/reshape | solution.py:68
  82.4 1.6 copy-done.1
  84.4 1.5 slice.12
  85.9 122.2 %reduce-scatter.4.cloned.1.call-done = f32[24,1344]{1,0:T(8,128)} async-done(((f32[384,1344]{1,0:T(8,128)}), f32[24,1344]{1,0:T(8,128)}) %reduce-scatter.4.cloned.1.call-update) | async-done | bytes 129040
  (30 shorter events, 1.9 us)
Async XLA Ops:
  6.5 49.6 %copy-start = (bf16[1,8,192,192]{3,2,1,0:T(8,128)(2,1)S(1)}, bf16[1,8,192,192]{3,2,1,0:T(8,128)(2,1)}, u32[]{:S(2)}) copy-start(bf16[1,8,192,192]{3,2,1,0:T(8,128)(2,1)} %param.6) | copy-start | bytes 1769476
  6.5 23.4 %copy-start.2 = (bf16[2,2,192,192]{3,2,1,0:T(8,128)(2,1)S(1)}, bf16[2,2,192,192]{3,2,1,0:T(8,128)(2,1)}, u32[]{:S(2)}) copy-start(bf16[2,2,192,192]{3,2,1,0:T(8,128)(2,1)} %param.10) | copy-start | bytes 884740
  6.5 201.6 %reduce-scatter.4.cloned.1.call-start = ((), (), s32[]{:S(2)}) async-start(), calls=%async_computation.1 | async-start | bytes 2297856
  6.5 45.4 %collective-permute-start.3 = (bf16[2,2,192,192]{3,2,1,0:T(8,128)(2,1)}, bf16[2,2,192,192]{3,2,1,0:T(8,128)(2,1)S(1)}, u32[]{:S(2)}, u32[]{:S(2)}) collective-permute-start(bf16[2,2,192,192]{3,2,1,0:T(8,128)(2,1)} %param.10), channel_id=1, source_target_pairs={{2,0},{3,1},{4,2},{5,3},{6,4},{7,5},{8,6},{9,7},{10,8},{11,9},{12,... | collective-permute-start | bytes 884744 | tf_op jit(solution)/shard_map/ppermute | solution.py:19
  16.4 34.8 %collective-permute-start.2 = (bf16[2,2,192,192]{3,2,1,0:T(8,128)(2,1)}, bf16[2,2,192,192]{3,2,1,0:T(8,128)(2,1)S(1)}, u32[]{:S(2)}, u32[]{:S(2)}) collective-permute-start(bf16[2,2,192,192]{3,2,1,0:T(8,128)(2,1)} %param.10), channel_id=1, source_target_pairs={{1,0},{2,1},{3,2},{4,3},{5,4},{6,5},{7,6},{8,7},{9,8},{10,9},{11,1... | collective-permute-start | bytes 884744 | tf_op jit(solution)/shard_map/ppermute | solution.py:19
  19.5 29.2 %collective-permute-start.1 = (bf16[2,2,192,192]{3,2,1,0:T(8,128)(2,1)}, bf16[2,2,192,192]{3,2,1,0:T(8,128)(2,1)}, u32[]{:S(2)}, u32[]{:S(2)}) collective-permute-start(bf16[2,2,192,192]{3,2,1,0:T(8,128)(2,1)} %param.10), channel_id=1, source_target_pairs={{0,1},{1,2},{2,3},{3,4},{4,5},{5,6},{6,7},{7,8},{8,9},{9,10},{10,1... | collective-permute-start | bytes 884744 | tf_op jit(solution)/shard_map/ppermute | solution.py:19
  21.7 25.2 %collective-permute-start = (bf16[2,2,192,192]{3,2,1,0:T(8,128)(2,1)}, bf16[2,2,192,192]{3,2,1,0:T(8,128)(2,1)}, u32[]{:S(2)}, u32[]{:S(2)}) collective-permute-start(bf16[2,2,192,192]{3,2,1,0:T(8,128)(2,1)} %param.10), channel_id=1, source_target_pairs={{0,2},{1,3},{2,4},{3,5},{4,6},{5,7},{6,8},{7,9},{8,10},{9,11},{10,... | collective-permute-start | bytes 884744 | tf_op jit(solution)/shard_map/ppermute | solution.py:19
  61.8 7.3 %copy-start.3 = (f32[3,7,8,2,2]{1,0,2,3,4:T(4,128)S(1)}, f32[3,7,8,2,2]{1,0,2,3,4:T(4,128)}, u32[]{:S(2)}) copy-start(f32[3,7,8,2,2]{1,0,2,3,4:T(4,128)} %reshape.211) | copy-start | bytes 8068
  82.1 1.9 copy-start.1
Sparse Core Ops, SparseCore 0:
  86.0 122.0 reduce-scatter.3
where the time goes:
time: 216 us; the launch traced here: 215 us
  waiting for transfers between devices  139 us (64%)
  local copies, waits for them, and re-layouts  29.2 us (14%)
  starting transfers between devices  17.7 us (8%)
  between operations  14.2 us (7%)
  matrix products  13.7 us (6%)
    unnamed x2, waiting for transfers between devices  122 us
    ppermute x4, starting transfers between devices, from_behind(): return lax.ppermute(value, axis, pairs)  17.7 us
    ppermute x4, waiting for transfers between devices, from_behind(): return lax.ppermute(value, axis, pairs)  16.3 us
    dot_general x1, matrix products, local(): gathered = jnp.einsum('sutq,sutwz->qwz', weights, triple, precision=HIGHEST)  7.98 us
    unnamed x13, local copies, waits for them, and re-layouts  7.82 us
    transpose x1, local copies, waits for them, and re-layouts, slot_triple(): jnp.einsum('suxw,stxz->sutwz', left_rows, product, preferred_element_type...  7.3 us
    dot_general x1, matrix products, slot_triple(): jnp.einsum('suxw,stxz->sutwz', left_rows, product, preferred_element_type...  5.7 us
    reshape x1, local copies, waits for them, and re-layouts, local(): flat = window.reshape(3, block_size, BAND * block_size)  5.04 us
  transfers between devices with their start and end apart: 5, of which 2 were waited for; matrix products, arithmetic and copies ran while one was open for 5% of the time, Pallas kernels for 0%

commit v1 on v0

v1 whole, which is shorter than its diff:
```python
import functools

import jax
import jax.numpy as jnp
from jax import lax
from jax.experimental import pallas as pl
from jax.experimental.pallas import tpu as pltpu
from jax.sharding import PartitionSpec as P

HB = 4
RB = 32
CR = 2
LANES = 128
CHUNKS = 3
MESH = pl.DeviceIdType.MESH
HALO = (1, -1, 2, -2)


def kernel(
    a_hbm, rows_hbm, cols_hbm, count_hbm, p_hbm, pc_hbm, out_ref,
    a_buf, p_buf, rows_s, cols_s, count_s, pc_s,
    own, halo0, halo1, halo2, stack, left, side_left, prod,
    mine, got0, got1, got2, side_mine, side_got0, side_got1, side_got2,
    load_sem, halo_send, halo_recv, band_send, band_recv, side_send, side_recv,
):
    rows_n, cols_n = lax.axis_size("row"), lax.axis_size("col")
    r, t = lax.axis_index("row"), lax.axis_index("col")
    slots, size = a_buf.shape[0], a_buf.shape[1]
    share = p_buf.shape[0]
    half = size - LANES
    piece = CR * size // cols_n
    halos, gots, side_gots = (halo0, halo1, halo2), (got0, got1, got2), (side_got0, side_got1, side_got2)
    first_row = r * RB + t * share
    aligned = pl.multiple_of(first_row // LANES * LANES, LANES)

    def shifted(by):
        flat = lax.rem(r * cols_n + t + by + rows_n * cols_n, rows_n * cols_n)
        return flat // cols_n, lax.rem(flat, cols_n)

    def peer(by):
        return r, lax.rem(t + by, cols_n)

    loads = [
        pltpu.make_async_copy(p_hbm, p_buf, load_sem.at[0]),
        pltpu.make_async_copy(pc_hbm.at[:, pl.ds(aligned, LANES)], pc_s, load_sem.at[1]),
        pltpu.make_async_copy(a_hbm.at[0], a_buf, load_sem.at[2]),
        pltpu.make_async_copy(rows_hbm, rows_s, load_sem.at[3]),
        pltpu.make_async_copy(cols_hbm, cols_s, load_sem.at[4]),
        pltpu.make_async_copy(count_hbm, count_s, load_sem.at[5]),
    ]
    for load in loads:
        load.start()

    barrier = pltpu.get_barrier_semaphore()
    for by in HALO:
        pl.semaphore_signal(barrier, inc=1, device_id=shifted(by), device_id_type=MESH)
    for by in range(1, cols_n):
        pl.semaphore_signal(barrier, inc=1, device_id=peer(by), device_id_type=MESH)

    loads[0].wait()
    loads[1].wait()
    for k in range(share):
        swap = jnp.clip(pc_s[0, first_row - aligned + k], 0, 1)
        low = p_buf[k, swap]
        high = p_buf[k, 1 - swap]
        parts = (low[:, :LANES], high[:, :LANES], jnp.concatenate([low[:, LANES:], high[:, LANES:]], axis=1))
        for c in range(CHUNKS):
            own[c, k] = parts[c]
            halos[c][HB + k] = parts[c]

    pl.semaphore_wait(barrier, len(HALO) + cols_n - 1)

    def halo_copy(c, n):
        by = HALO[n]
        return pltpu.make_async_remote_copy(
            src_ref=own.at[c],
            dst_ref=halos[c].at[pl.ds(HB - share * by, share)],
            send_sem=halo_send.at[c, n],
            recv_sem=halo_recv.at[c, n],
            device_id=shifted(by),
            device_id_type=MESH,
        )

    for c in range(CHUNKS):
        for n in range(len(HALO)):
            halo_copy(c, n).start()

    for load in loads[2:]:
        load.wait()
    edge = (t < 2) | (t >= cols_n - 2)
    total_rows = rows_n * RB
    count = count_s[0, 0]
    picks = []
    for s in range(slots):
        column = cols_s[0, s]
        row = (r - 1) * RB + column
        live = (count > s) & (row >= 0) & (row < total_rows)
        centre = (column >= RB) & (column < 2 * RB)
        picks.append(jnp.clip(column - RB - t * share + HB, 0, halo0.shape[0] - 1))
        line = jnp.clip(rows_s[0, s] - t * share, 0, share - 1)
        for c in range(CHUNKS):
            value = own[c, line]
            zero = jnp.zeros_like(value)
            stack[c, s * size : (s + 1) * size, :] = jnp.where(live & centre, value, zero)

    def turn(into):
        flips = [stack[c].T for c in range(CHUNKS)]
        into[0:LANES, :] = flips[0]
        into[LANES:size, :] = flips[2][:half]
        into[size : size + LANES, :] = flips[1]
        into[size + LANES :, :] = flips[2][half:]

    turn(left)

    @pl.when(edge)
    def _():
        for s in range(slots):
            column = cols_s[0, s]
            row = (r - 1) * RB + column
            live = (count > s) & (row >= 0) & (row < total_rows)
            outside = (column < RB) | (column >= 2 * RB)
            line = jnp.clip(rows_s[0, s] - t * share, 0, share - 1)
            for c in range(CHUNKS):
                value = own[c, line]
                zero = jnp.zeros_like(value)
                stack[c, s * size : (s + 1) * size, :] = jnp.where(live & outside, value, zero)
        turn(side_left)

    side_slot = jnp.where(t < 2, t, t - cols_n + 4)

    def pieces(value):
        value = value.reshape(cols_n, piece, LANES)
        pad = jnp.zeros((cols_n, mine.shape[2] - piece, LANES), value.dtype)
        return jnp.concatenate([value, pad], axis=1).astype(mine.dtype)

    def band_copy(c, by):
        return pltpu.make_async_remote_copy(
            src_ref=mine.at[c, lax.rem(t + by, cols_n)],
            dst_ref=gots[c].at[t],
            send_sem=band_send.at[c],
            recv_sem=band_recv.at[c],
            device_id=peer(by),
            device_id_type=MESH,
        )

    def side_copy(c, by):
        return pltpu.make_async_remote_copy(
            src_ref=side_mine.at[c, lax.rem(t + by, cols_n)],
            dst_ref=side_gots[c].at[side_slot],
            send_sem=side_send.at[c],
            recv_sem=side_recv.at[c],
            device_id=peer(by),
            device_id_type=MESH,
        )

    for c in range(CHUNKS):
        for n in range(len(HALO)):
            halo_copy(c, n).wait_recv()
        for s in range(slots):
            value = jnp.dot(a_buf[s], halos[c][picks[s]], preferred_element_type=jnp.float32)
            prod[s * size : (s + 1) * size, :] = value.astype(prod.dtype)
        mine[c] = pieces(jnp.dot(left[...], prod[...], preferred_element_type=jnp.float32))
        for by in range(1, cols_n):
            band_copy(c, by).start()
        gots[c][t] = mine[c, t]

        @pl.when(edge)
        def _():
            side_mine[c] = pieces(jnp.dot(side_left[...], prod[...], preferred_element_type=jnp.float32))
            for by in range(1, cols_n):
                side_copy(c, by).start()
            side_gots[c][side_slot] = side_mine[c, t]

    for c in range(CHUNKS):
        for n in range(len(HALO)):
            halo_copy(c, n).wait_send()

    sums = []
    for c in range(CHUNKS):
        everyone = pl.ds(0, cols_n - 1)
        pltpu.make_async_copy(gots[c].at[everyone], gots[c].at[everyone], band_recv.at[c]).wait()

        @pl.when(edge)
        def _():
            pltpu.make_async_copy(side_gots[c].at[pl.ds(0, 3)], side_gots[c].at[pl.ds(0, 3)], side_recv.at[c]).wait()

        @pl.when(jnp.logical_not(edge))
        def _():
            pltpu.make_async_copy(side_gots[c], side_gots[c], side_recv.at[c]).wait()

        centre = jnp.sum(gots[c][...].astype(jnp.float32), axis=0)[:piece]
        sides = side_gots[c][...].astype(jnp.float32)
        sums.append(((sides[0] + sides[1])[:piece], centre, (sides[2] + sides[3])[:piece]))

    for c in range(CHUNKS):
        everyone = pl.ds(0, cols_n - 1)
        pltpu.make_async_copy(mine.at[c, everyone], mine.at[c, everyone], band_send.at[c]).wait()

        @pl.when(edge)
        def _():
            pltpu.make_async_copy(side_mine.at[c, everyone], side_mine.at[c, everyone], side_send.at[c]).wait()

    blocks = []
    for j in range(3):
        first, second, mixed = sums[0][j], sums[1][j], sums[2][j]
        blocks += [first, mixed[:, :half], second, mixed[:, half:]]
    empty = jnp.zeros((piece, size), jnp.float32)

    @pl.when(t < cols_n // CR)
    def _():
        out_ref[...] = jnp.concatenate([empty] + blocks, axis=1)

    @pl.when(t >= cols_n // CR)
    def _():
        out_ref[...] = jnp.concatenate(blocks + [empty], axis=1)


def local(a_vals, a_rows, a_cols, a_count, p_vals, p_cols):
    slots, size = a_vals.shape[1], a_vals.shape[2]
    share = p_vals.shape[0]
    cols_n = lax.axis_size("col")
    piece = CR * size // cols_n
    padded = -(-piece // 16) * 16
    width = share + 2 * HB
    kind = p_vals.dtype
    anywhere = pl.BlockSpec(memory_space=pltpu.HBM)
    halo = pltpu.VMEM((width, size, LANES), kind)
    got = pltpu.VMEM((cols_n, padded, LANES), kind)
    side_got = pltpu.VMEM((4, padded, LANES), kind)
    return pl.pallas_call(
        kernel,
        out_shape=jax.ShapeDtypeStruct((piece, 7 * size), jnp.float32),
        in_specs=[anywhere] * 6,
        out_specs=pl.BlockSpec(memory_space=pltpu.VMEM),
        scratch_shapes=[
            pltpu.VMEM((slots, size, size), kind),
            pltpu.VMEM((share, 2, size, size), kind),
            pltpu.SMEM((1, slots), jnp.int32),
            pltpu.SMEM((1, slots), jnp.int32),
            pltpu.SMEM((1, 1), jnp.int32),
            pltpu.SMEM((2, LANES), jnp.int32),
            pltpu.VMEM((CHUNKS, share, size, LANES), kind),
            halo, halo, halo,
            pltpu.VMEM((CHUNKS, slots * size, LANES), kind),
            pltpu.VMEM((CR * size, slots * size), kind),
            pltpu.VMEM((CR * size, slots * size), kind),
            pltpu.VMEM((slots * size, LANES), kind),
            pltpu.VMEM((CHUNKS, cols_n, padded, LANES), kind),
            got, got, got,
            pltpu.VMEM((CHUNKS, cols_n, padded, LANES), kind),
            side_got, side_got, side_got,
            pltpu.SemaphoreType.DMA((6,)),
            pltpu.SemaphoreType.DMA((CHUNKS, len(HALO))),
            pltpu.SemaphoreType.DMA((CHUNKS, len(HALO))),
            pltpu.SemaphoreType.DMA((CHUNKS,)),
            pltpu.SemaphoreType.DMA((CHUNKS,)),
            pltpu.SemaphoreType.DMA((CHUNKS,)),
            pltpu.SemaphoreType.DMA((CHUNKS,)),
        ],
        compiler_params=pltpu.CompilerParams(
            collective_id=0, has_side_effects=True, vmem_limit_bytes=62 * 2**20
        ),
        name="galerkin",
    )(a_vals, a_rows, a_cols, a_count, p_vals, p_cols.T)


def solution(mesh):
    placed = (
        P("row", "col", None, None),
        P("row", "col"),
        P("row", "col"),
        P("row", "col"),
        P(("row", "col"), None, None, None),
        P(),
    )
    return jax.shard_map(
        local, mesh=mesh, in_specs=placed, out_specs=P(("row", "col"), None), check_vma=False
    )
```

time: 216 us -> 56.9 us (0.26)
  the two profiles are of different devices: /device:TPU:1 before, /device:TPU:8 now
where the time goes in v1:
time: 56.9 us; the launch traced here: 56.7 us
  Pallas kernels  54.5 us (96%)
  local copies, waits for them, and re-layouts  1.57 us (3%)
  between operations  0.66 us (1%)
    pallas_call x1, Pallas kernels, local(): pl.pallas_call(kernel, out_shape=jax.ShapeDtypeStruct((piece, 7 * size),...  54.5 us
    unnamed x1, local copies, waits for them, and re-layouts  1.57 us

profile of v1, /device:TPU:8, one launch (start us, length us, event | category | flops | bytes accessed | tf_op | source)
XLA Modules:
  0.0 56.7 jit_solution(8999921012592510164)
XLA Ops:
  0.7 54.5 %galerkin.1 = f32[24,1344]{1,0:T(8,128)} custom-call(bf16[1,8,192,192]{3,2,1,0:T(8,128)(2,1)} %a_hbm.1, s32[1,8]{1,0:T(1,128)} %rows_hbm.1, s32[1,8]{1,0:T(1,128)} %cols_hbm.1, s32[1,1]{1,0:T(1,128)S(6)} %copy.8.count_hbm, bf16[2,2,192,192]{3,2,1,0:T(8,128)(2,1)} %p_hbm.1, s32[2,2048]{1,0:T(2,128)} %bitcast.1), custom_call_target="tpu_custom_call" | custom-call | tf_op jit(solution)/shard_map/galerkin/pallas_call | solution.py:230
  55.1 1.6 %copy.9 = f32[24,1344]{1,0:T(8,128)} copy(f32[24,1344]{1,0:T(8,128)} %galerkin.1) | data formatting | bytes 258048

commit v2 on v1

v2 whole, which is shorter than its diff:
```python
import functools

import jax
import jax.numpy as jnp
from jax import lax
from jax.experimental import pallas as pl
from jax.experimental.pallas import tpu as pltpu
from jax.sharding import PartitionSpec as P

HB = 4
RB = 32
CR = 2
LANES = 128
CHUNKS = 3
MESH = pl.DeviceIdType.MESH
SPAN = 4


def kernel(
    a_hbm, rows_hbm, cols_hbm, count_hbm, p_hbm, pc_hbm, out_ref,
    a_buf, p_buf, rows_s, cols_s, count_s, pc_s,
    own, halo0, halo1, halo2, relay, stack, left, side_left, prod,
    mine, got0, got1, got2, side_mine, side_got0, side_got1, side_got2,
    part, lined0, lined1, lined2, side_part, side_lined0, side_lined1, side_lined2,
    load_sem, halo_send, halo_recv, relay_send, relay_recv, skip_send,
    band_send, band_recv, side_send, side_recv, line_send, line_recv, side_line_send, side_line_recv,
):
    rows_n, cols_n = lax.axis_size("row"), lax.axis_size("col")
    r, t = lax.axis_index("row"), lax.axis_index("col")
    slots, size = a_buf.shape[0], a_buf.shape[1]
    share = p_buf.shape[0]
    half = size - LANES
    piece = CR * size // cols_n
    lined, side_lined = (lined0, lined1, lined2), (side_lined0, side_lined1, side_lined2)
    halos, gots, side_gots = (halo0, halo1, halo2), (got0, got1, got2), (side_got0, side_got1, side_got2)
    first_row = r * RB + t * share
    aligned = pl.multiple_of(first_row // LANES * LANES, LANES)

    def shifted(by):
        flat = lax.rem(r * cols_n + t + by + rows_n * cols_n, rows_n * cols_n)
        return flat // cols_n, lax.rem(flat, cols_n)

    lines = cols_n // SPAN
    place, line_of = lax.rem(t, SPAN), t // SPAN
    first, last = place == 0, place == SPAN - 1

    def beside(by):
        return r, line_of * SPAN + lax.rem(place + by, SPAN)

    def above(by):
        return r, lax.rem(t + by * SPAN, cols_n)

    loads = [
        pltpu.make_async_copy(p_hbm, p_buf, load_sem.at[0]),
        pltpu.make_async_copy(pc_hbm.at[:, pl.ds(aligned, LANES)], pc_s, load_sem.at[1]),
        pltpu.make_async_copy(a_hbm.at[0], a_buf, load_sem.at[2]),
        pltpu.make_async_copy(rows_hbm, rows_s, load_sem.at[3]),
        pltpu.make_async_copy(cols_hbm, cols_s, load_sem.at[4]),
        pltpu.make_async_copy(count_hbm, count_s, load_sem.at[5]),
    ]
    for load in loads:
        load.start()

    barrier = pltpu.get_barrier_semaphore()
    friends = [shifted(by) for by in (1, -1, 2, -2, SPAN, -SPAN)]
    friends += [beside(by) for by in range(1, SPAN)] + [above(by) for by in range(1, lines)]
    for friend in friends:
        pl.semaphore_signal(barrier, inc=1, device_id=friend, device_id_type=MESH)

    loads[0].wait()
    loads[1].wait()
    for k in range(share):
        swap = jnp.clip(pc_s[0, first_row - aligned + k], 0, 1)
        low = p_buf[k, swap]
        high = p_buf[k, 1 - swap]
        parts = (low[:, :LANES], high[:, :LANES], jnp.concatenate([low[:, LANES:], high[:, LANES:]], axis=1))
        for c in range(CHUNKS):
            own[c, k] = parts[c]
            halos[c][HB + k] = parts[c]

    pl.semaphore_wait(barrier, len(friends))

    def halo_copy(source, target, device, sent, landed):
        return pltpu.make_async_remote_copy(
            src_ref=source,
            dst_ref=target,
            send_sem=sent,
            recv_sem=landed,
            device_id=device,
            device_id_type=MESH,
        )

    def rows_at(c, start):
        return halos[c].at[pl.ds(start, share)]

    def near_copy(c, n):
        by = 1 - 2 * n
        return halo_copy(
            own.at[c], rows_at(c, HB - share * by), shifted(by), halo_send.at[c, n], halo_recv.at[c, n]
        )

    def far_copy(c, n):
        by = 1 - 2 * n
        source, target = rows_at(c, HB - share * by), rows_at(c, HB - 2 * share * by)
        return halo_copy(source, target, shifted(by), halo_send.at[c, 2 + n], halo_recv.at[c, 2 + n])

    def to_relay(c, n):
        by = 1 - 2 * n
        across = r, t - (SPAN - 1) * by
        source = rows_at(c, HB - share * by)
        return halo_copy(source, relay.at[c], across, halo_send.at[c, 2 + n], relay_recv.at[c])

    def from_relay(c, n):
        by = 1 - 2 * n
        target = rows_at(c, HB - 2 * share * by)
        return halo_copy(relay.at[c], target, shifted(SPAN * by), relay_send.at[c], halo_recv.at[c, 2 + n])

    def skip_copy(n):
        by = 1 - 2 * n
        target = rows_at(0, HB - 2 * share * by)
        return halo_copy(own.at[0], target, shifted(2 * by), skip_send, halo_recv.at[0, 2 + n])

    def pass_on(c):
        for n, turning in ((0, last), (1, first)):
            near_copy(c, n).wait_recv()

            if c > 0:

                @pl.when(turning)
                def _():
                    to_relay(c, n).start()

            @pl.when(jnp.logical_not(turning))
            def _():
                far_copy(c, n).start()

    def pass_relay(c):
        for n, turning in ((0, first), (1, last)):

            @pl.when(turning)
            def _():
                to_relay(c, n).wait_recv()
                from_relay(c, n).start()

    skips = (place == SPAN - 2, place == 1)
    for c in range(2):
        for n in range(2):
            near_copy(c, n).start()

            if c == 0:

                @pl.when(skips[n])
                def _():
                    skip_copy(n).start()

    for load in loads[2:]:
        load.wait()
    edge = (t < 2) | (t >= cols_n - 2)
    total_rows = rows_n * RB
    count = count_s[0, 0]
    picks = []
    for s in range(slots):
        column = cols_s[0, s]
        row = (r - 1) * RB + column
        live = (count > s) & (row >= 0) & (row < total_rows)
        centre = (column >= RB) & (column < 2 * RB)
        picks.append(jnp.clip(column - RB - t * share + HB, 0, halo0.shape[0] - 1))
        line = jnp.clip(rows_s[0, s] - t * share, 0, share - 1)
        for c in range(CHUNKS):
            value = own[c, line]
            zero = jnp.zeros_like(value)
            stack[c, s * size : (s + 1) * size, :] = jnp.where(live & centre, value, zero)

    def turn(into):
        flips = [stack[c].T for c in range(CHUNKS)]
        into[0:LANES, :] = flips[0]
        into[LANES:size, :] = flips[2][:half]
        into[size : size + LANES, :] = flips[1]
        into[size + LANES :, :] = flips[2][half:]

    pass_on(0)
    for n in range(2):
        near_copy(2, n).start()
    turn(left)
    pass_on(1)

    @pl.when(edge)
    def _():
        for s in range(slots):
            column = cols_s[0, s]
            row = (r - 1) * RB + column
            live = (count > s) & (row >= 0) & (row < total_rows)
            outside = (column < RB) | (column >= 2 * RB)
            line = jnp.clip(rows_s[0, s] - t * share, 0, share - 1)
            for c in range(CHUNKS):
                value = own[c, line]
                zero = jnp.zeros_like(value)
                stack[c, s * size : (s + 1) * size, :] = jnp.where(live & outside, value, zero)
        turn(side_left)

    pass_relay(1)
    pass_on(2)
    def pieces(value):
        value = value.reshape(lines, SPAN, piece, LANES)
        value = jnp.stack([value[:, k] for k in range(SPAN)])
        return value.reshape(SPAN, lines * piece, LANES).astype(mine.dtype)

    def band_copy(c, by):
        device = beside(by)
        return pltpu.make_async_remote_copy(
            src_ref=mine.at[c, lax.rem(place + by, SPAN)],
            dst_ref=gots[c].at[place],
            send_sem=band_send.at[c],
            recv_sem=band_recv.at[c],
            device_id=device,
            device_id_type=MESH,
        )

    def side_copy(c, by):
        return pltpu.make_async_remote_copy(
            src_ref=side_mine.at[c, lax.rem(place + by, SPAN)],
            dst_ref=side_gots[c].at[lax.rem(t, 2)],
            send_sem=side_send.at[c],
            recv_sem=side_recv.at[c],
            device_id=beside(by),
            device_id_type=MESH,
        )

    def line_copy(c, by):
        return pltpu.make_async_remote_copy(
            src_ref=part.at[c, lax.rem(line_of + by, lines)],
            dst_ref=lined[c].at[line_of],
            send_sem=line_send.at[c],
            recv_sem=line_recv.at[c],
            device_id=above(by),
            device_id_type=MESH,
        )

    def side_line_copy(c, by):
        return pltpu.make_async_remote_copy(
            src_ref=side_part.at[c, lax.rem(line_of + by, lines)],
            dst_ref=side_lined[c].at[line_of // (lines - 1)],
            send_sem=side_line_send.at[c],
            recv_sem=side_line_recv.at[c, line_of // (lines - 1)],
            device_id=above(by),
            device_id_type=MESH,
        )

    def landed(ref, count, sem):
        some = ref.at[pl.ds(0, count)]
        pltpu.make_async_copy(some, some, sem).wait()

    outer = (line_of == 0) | (line_of == lines - 1)

    def work(c):
        for n in range(2):
            far_copy(c, n).wait_recv()
        for s in range(slots):
            value = jnp.dot(a_buf[s], halos[c][picks[s]], preferred_element_type=jnp.float32)
            prod[s * size : (s + 1) * size, :] = value.astype(prod.dtype)
        mine[c] = pieces(jnp.dot(left[...], prod[...], preferred_element_type=jnp.float32))
        for by in range(1, SPAN):
            band_copy(c, by).start()
        gots[c][place] = mine[c, place]

        @pl.when(edge)
        def _():
            side_mine[c] = pieces(jnp.dot(side_left[...], prod[...], preferred_element_type=jnp.float32))
            for by in range(1, SPAN):
                side_copy(c, by).start()
            side_gots[c][lax.rem(t, 2)] = side_mine[c, place]

    def hand_on(c):
        landed(gots[c], SPAN - 1, band_recv.at[c])
        total = jnp.sum(gots[c][...].astype(jnp.float32), axis=0).reshape(lines, piece, LANES)
        part[c] = total
        for by in range(1, lines):
            line_copy(c, by).start()
        lined[c][line_of] = part[c, line_of]

        @pl.when(outer)
        def _():
            @pl.when(edge)
            def _():
                landed(side_gots[c], 1, side_recv.at[c])

            @pl.when(jnp.logical_not(edge))
            def _():
                landed(side_gots[c], 2, side_recv.at[c])

            sides = side_gots[c][...].astype(jnp.float32)
            side_part[c] = (sides[0] + sides[1]).reshape(lines, piece, LANES)
            for by in range(1, lines):
                side_line_copy(c, by).start()
            side_lined[c][line_of // (lines - 1)] = side_part[c, line_of]

    work(0)
    pass_relay(2)
    work(1)
    hand_on(0)
    work(2)
    hand_on(1)
    hand_on(2)
    for c in range(CHUNKS):
        for n in range(2):
            near_copy(c, n).wait_send()
            if c > 0:
                far_copy(c, n).wait_send()

                @pl.when((first, last)[n])
                def _():
                    from_relay(c, n).wait_send()

            else:

                @pl.when(jnp.logical_not((last, first)[n]))
                def _():
                    far_copy(c, n).wait_send()

                @pl.when(skips[n])
                def _():
                    skip_copy(n).wait_send()

    sums = []
    for c in range(CHUNKS):
        landed(lined[c], lines - 1, line_recv.at[c])
        for k in range(2):

            @pl.when(line_of != k * (lines - 1))
            def _():
                landed(side_lined[c], 1, side_line_recv.at[c, k])

        sums.append((side_lined[c][0], jnp.sum(lined[c][...], axis=0), side_lined[c][1]))

    for c in range(CHUNKS):
        landed(mine.at[c], SPAN - 1, band_send.at[c])
        landed(part.at[c], lines - 1, line_send.at[c])

        @pl.when(edge)
        def _():
            landed(side_mine.at[c], SPAN - 1, side_send.at[c])

        @pl.when(outer)
        def _():
            landed(side_part.at[c], lines - 1, side_line_send.at[c])

    blocks = []
    for j in range(3):
        low, high, mixed = sums[0][j], sums[1][j], sums[2][j]
        blocks += [low, mixed[:, :half], high, mixed[:, half:]]
    empty = jnp.zeros((piece, size), jnp.float32)

    @pl.when(t < cols_n // CR)
    def _():
        out_ref[...] = jnp.concatenate([empty] + blocks, axis=1)

    @pl.when(t >= cols_n // CR)
    def _():
        out_ref[...] = jnp.concatenate(blocks + [empty], axis=1)


def local(a_vals, a_rows, a_cols, a_count, p_vals, p_cols):
    slots, size = a_vals.shape[1], a_vals.shape[2]
    share = p_vals.shape[0]
    cols_n = lax.axis_size("col")
    piece = CR * size // cols_n
    lines = cols_n // SPAN
    width = share + 2 * HB
    kind = p_vals.dtype
    anywhere = pl.BlockSpec(memory_space=pltpu.HBM)
    halo = pltpu.VMEM((width, size, LANES), kind)
    got = pltpu.VMEM((SPAN, lines * piece, LANES), kind)
    side_got = pltpu.VMEM((2, lines * piece, LANES), kind)
    lined = pltpu.VMEM((lines, piece, LANES), jnp.float32)
    side_lined = pltpu.VMEM((2, piece, LANES), jnp.float32)
    return pl.pallas_call(
        kernel,
        out_shape=jax.ShapeDtypeStruct((piece, 7 * size), jnp.float32),
        in_specs=[anywhere] * 6,
        out_specs=pl.BlockSpec(memory_space=pltpu.VMEM),
        scratch_shapes=[
            pltpu.VMEM((slots, size, size), kind),
            pltpu.VMEM((share, 2, size, size), kind),
            pltpu.SMEM((1, slots), jnp.int32),
            pltpu.SMEM((1, slots), jnp.int32),
            pltpu.SMEM((1, 1), jnp.int32),
            pltpu.SMEM((2, LANES), jnp.int32),
            pltpu.VMEM((CHUNKS, share, size, LANES), kind),
            halo, halo, halo,
            pltpu.VMEM((CHUNKS, share, size, LANES), kind),
            pltpu.VMEM((CHUNKS, slots * size, LANES), kind),
            pltpu.VMEM((CR * size, slots * size), kind),
            pltpu.VMEM((CR * size, slots * size), kind),
            pltpu.VMEM((slots * size, LANES), kind),
            pltpu.VMEM((CHUNKS, SPAN, lines * piece, LANES), kind),
            got, got, got,
            pltpu.VMEM((CHUNKS, SPAN, lines * piece, LANES), kind),
            side_got, side_got, side_got,
            pltpu.VMEM((CHUNKS, lines, piece, LANES), jnp.float32),
            lined, lined, lined,
            pltpu.VMEM((CHUNKS, lines, piece, LANES), jnp.float32),
            side_lined, side_lined, side_lined,
            pltpu.SemaphoreType.DMA((6,)),
            pltpu.SemaphoreType.DMA((CHUNKS, 4)),
            pltpu.SemaphoreType.DMA((CHUNKS, 4)),
            pltpu.SemaphoreType.DMA((CHUNKS,)),
            pltpu.SemaphoreType.DMA((CHUNKS,)),
            pltpu.SemaphoreType.DMA,
        ]
        + [pltpu.SemaphoreType.DMA((CHUNKS,))] * 7
        + [pltpu.SemaphoreType.DMA((CHUNKS, 2))],
        compiler_params=pltpu.CompilerParams(
            collective_id=0, has_side_effects=True, vmem_limit_bytes=62 * 2**20
        ),
        name="galerkin",
    )(a_vals, a_rows, a_cols, a_count, p_vals, p_cols.T)


def solution(mesh):
    placed = (
        P("row", "col", None, None),
        P("row", "col"),
        P("row", "col"),
        P("row", "col"),
        P(("row", "col"), None, None, None),
        P(),
    )
    return jax.shard_map(
        local, mesh=mesh, in_specs=placed, out_specs=P(("row", "col"), None), check_vma=False
    )
```

time: 56.9 us -> 53.2 us (0.935)
  the two profiles are of different devices: /device:TPU:8 before, /device:TPU:20 now
where the time goes in v2:
time: 53.2 us; the launch traced here: 53.1 us
  Pallas kernels  50.8 us (95%)
  local copies, waits for them, and re-layouts  1.57 us (3%)
  between operations  0.66 us (1%)
    pallas_call x1, Pallas kernels, local(): pl.pallas_call(kernel, out_shape=jax.ShapeDtypeStruct((piece, 7 * size),...  50.8 us
    unnamed x1, local copies, waits for them, and re-layouts  1.57 us

profile of v2, /device:TPU:20, one launch (start us, length us, event | category | flops | bytes accessed | tf_op | source)
XLA Modules:
  0.0 53.1 jit_solution(8358393260075251363)
XLA Ops:
  0.7 50.8 %galerkin.1 = f32[24,1344]{1,0:T(8,128)} custom-call(bf16[1,8,192,192]{3,2,1,0:T(8,128)(2,1)} %a_hbm.1, s32[1,8]{1,0:T(1,128)} %rows_hbm.1, s32[1,8]{1,0:T(1,128)} %cols_hbm.1, s32[1,1]{1,0:T(1,128)S(6)} %copy.8.count_hbm, bf16[2,2,192,192]{3,2,1,0:T(8,128)(2,1)} %p_hbm.1, s32[2,2048]{1,0:T(2,128)} %bitcast.1), custom_call_target="tpu_custom_call" | custom-call | tf_op jit(solution)/shard_map/galerkin/pallas_call | solution.py:376
  51.5 1.6 %copy.9 = f32[24,1344]{1,0:T(8,128)} copy(f32[24,1344]{1,0:T(8,128)} %galerkin.1) | data formatting | bytes 258048

commit v3 on v2

--- a/solution.py
+++ b/solution.py
@@ -36,9 +36,15 @@
     first_row = r * RB + t * share
     aligned = pl.multiple_of(first_row // LANES * LANES, LANES)
 
+    flat = r * cols_n + t
+    tiles = rows_n * cols_n
+
+    def within(by):
+        return (flat + by >= 0) & (flat + by < tiles)
+
     def shifted(by):
-        flat = lax.rem(r * cols_n + t + by + rows_n * cols_n, rows_n * cols_n)
-        return flat // cols_n, lax.rem(flat, cols_n)
+        other = lax.rem(flat + by + tiles, tiles)
+        return other // cols_n, lax.rem(other, cols_n)
 
     lines = cols_n // SPAN
     place, line_of = lax.rem(t, SPAN), t // SPAN
@@ -62,10 +68,16 @@
         load.start()
 
     barrier = pltpu.get_barrier_semaphore()
-    friends = [shifted(by) for by in (1, -1, 2, -2, SPAN, -SPAN)]
-    friends += [beside(by) for by in range(1, SPAN)] + [above(by) for by in range(1, lines)]
+    friends = [beside(by) for by in range(1, SPAN)] + [above(by) for by in range(1, lines)]
     for friend in friends:
         pl.semaphore_signal(barrier, inc=1, device_id=friend, device_id_type=MESH)
+    expected = jnp.int32(len(friends))
+    for by in (1, -1, 2, -2, SPAN, -SPAN):
+        expected += within(by).astype(jnp.int32)
+
+        @pl.when(within(by))
+        def _():
+            pl.semaphore_signal(barrier, inc=1, device_id=shifted(by), device_id_type=MESH)
 
     loads[0].wait()
     loads[1].wait()
@@ -78,7 +90,17 @@
             own[c, k] = parts[c]
             halos[c][HB + k] = parts[c]
 
-    pl.semaphore_wait(barrier, len(friends))
+    for n in range(2):
+        by = 1 - 2 * n
+        for far in (1, 2):
+
+            @pl.when(jnp.logical_not(within(-far * by)))
+            def _():
+                for c in range(CHUNKS):
+                    empty_rows = jnp.zeros((share, size, LANES), halos[c].dtype)
+                    halos[c][HB - far * share * by : HB - far * share * by + share] = empty_rows
+
+    pl.semaphore_wait(barrier, expected)
 
     def halo_copy(source, target, device, sent, landed):
         return pltpu.make_async_remote_copy(
@@ -117,41 +139,69 @@
 
     def skip_copy(n):
         by = 1 - 2 * n
-        target = rows_at(0, HB - 2 * share * by)
-        return halo_copy(own.at[0], target, shifted(2 * by), skip_send, halo_recv.at[0, 2 + n])
-
-    def pass_on(c):
-        for n, turning in ((0, last), (1, first)):
-            near_copy(c, n).wait_recv()
-
-            if c > 0:
-
-                @pl.when(turning)
+        c = CHUNKS - 1
+        target = rows_at(c, HB - 2 * share * by)
+        return halo_copy(own.at[c], target, shifted(2 * by), skip_send, halo_recv.at[c, 2 + n])
+
+    turning, late, skips = (last, first), (first, last), (place == SPAN - 2, place == 1)
+    ahead, behind = (within(1), within(-1)), (within(-1), within(1))
+    skips = tuple(skips[n] & within(2 - 4 * n) for n in range(2))
+    relaying = tuple(late[n] & within(SPAN * (1 - 2 * n)) for n in range(2))
+    far_on = tuple(jnp.logical_not(turning[n]) & behind[n] & ahead[n] for n in range(2))
+    relay_on = tuple(turning[n] & ahead[n] for n in range(2))
+
+    def pass_fast(c):
+        for n in range(2):
+
+            @pl.when(jnp.logical_not(late[n]))
+            def _():
+                near_copy(c, n).wait_recv()
+
+                @pl.when(far_on[n])
                 def _():
-                    to_relay(c, n).start()
-
-            @pl.when(jnp.logical_not(turning))
-            def _():
-                far_copy(c, n).start()
+                    far_copy(c, n).start()
+
+                if c < CHUNKS - 1:
+
+                    @pl.when(relay_on[n])
+                    def _():
+                        to_relay(c, n).start()
+
+    def pass_late(c):
+        for n in range(2):
+
+            @pl.when(late[n] & behind[n])
+            def _():
+                near_copy(c, n).wait_recv()
+
+                @pl.when(far_on[n])
+                def _():
+                    far_copy(c, n).start()
 
     def pass_relay(c):
-        for n, turning in ((0, first), (1, last)):
-
-            @pl.when(turning)
+        for n in range(2):
+
+            @pl.when(relaying[n])
             def _():
                 to_relay(c, n).wait_recv()
                 from_relay(c, n).start()
 
-    skips = (place == SPAN - 2, place == 1)
-    for c in range(2):
-        for n in range(2):
-            near_copy(c, n).start()
-
-            if c == 0:
-
-                @pl.when(skips[n])
-                def _():
-                    skip_copy(n).start()
+    for c in range(CHUNKS - 1):
+        for n in range(2):
+
+            @pl.when(ahead[n])
+            def _():
+                near_copy(c, n).start()
+
+    for n in range(2):
+
+        @pl.when(skips[n])
+        def _():
+            skip_copy(n).start()
+
+        @pl.when(jnp.logical_not(turning[n]) & ahead[n])
+        def _():
+            near_copy(CHUNKS - 1, n).start()
 
     for load in loads[2:]:
         load.wait()
@@ -178,11 +228,18 @@
         into[size : size + LANES, :] = flips[1]
         into[size + LANES :, :] = flips[2][half:]
 
-    pass_on(0)
+    turn(left)
+    pass_fast(0)
+    pass_fast(1)
     for n in range(2):
-        near_copy(2, n).start()
-    turn(left)
-    pass_on(1)
+
+        @pl.when(relay_on[n])
+        def _():
+            near_copy(CHUNKS - 1, n).start()
+
+    pass_relay(0)
+    pass_fast(2)
+    pass_relay(1)
 
     @pl.when(edge)
     def _():
@@ -198,8 +255,6 @@
                 stack[c, s * size : (s + 1) * size, :] = jnp.where(live & outside, value, zero)
         turn(side_left)
 
-    pass_relay(1)
-    pass_on(2)
     def pieces(value):
         value = value.reshape(lines, SPAN, piece, LANES)
         value = jnp.stack([value[:, k] for k in range(SPAN)])
@@ -254,7 +309,11 @@
 
     def work(c):
         for n in range(2):
-            far_copy(c, n).wait_recv()
+
+            @pl.when(within(4 * n - 2))
+            def _():
+                far_copy(c, n).wait_recv()
+
         for s in range(slots):
             value = jnp.dot(a_buf[s], halos[c][picks[s]], preferred_element_type=jnp.float32)
             prod[s * size : (s + 1) * size, :] = value.astype(prod.dtype)
@@ -294,8 +353,10 @@
                 side_line_copy(c, by).start()
             side_lined[c][line_of // (lines - 1)] = side_part[c, line_of]
 
+    pass_late(0)
+    pass_late(1)
     work(0)
-    pass_relay(2)
+    pass_late(2)
     work(1)
     hand_on(0)
     work(2)
@@ -303,19 +364,26 @@
     hand_on(2)
     for c in range(CHUNKS):
         for n in range(2):
-            near_copy(c, n).wait_send()
-            if c > 0:
+
+            @pl.when(ahead[n])
+            def _():
+                near_copy(c, n).wait_send()
+
+            @pl.when(far_on[n])
+            def _():
                 far_copy(c, n).wait_send()
 
-                @pl.when((first, last)[n])
+            if c < CHUNKS - 1:
+
+                @pl.when(relay_on[n])
+                def _():
+                    to_relay(c, n).wait_send()
+
+                @pl.when(relaying[n])
                 def _():
                     from_relay(c, n).wait_send()
 
             else:
-
-                @pl.when(jnp.logical_not((last, first)[n]))
-                def _():
-                    far_copy(c, n).wait_send()
 
                 @pl.when(skips[n])
                 def _():

time: 53.2 us -> 48.8 us (0.917)
  the two profiles are of different devices: /device:TPU:20 before, /device:TPU:960 now
where the time goes in v3:
time: 48.8 us; the launch traced here: 48.6 us
  Pallas kernels  46.4 us (95%)
  local copies, waits for them, and re-layouts  1.57 us (3%)
  between operations  0.66 us (1%)
    pallas_call x1, Pallas kernels, local(): pl.pallas_call(kernel, out_shape=jax.ShapeDtypeStruct((piece, 7 * size),...  46.4 us
    unnamed x1, local copies, waits for them, and re-layouts  1.57 us

profile of v3, /device:TPU:960, one launch (start us, length us, event | category | flops | bytes accessed | tf_op | source)
XLA Modules:
  0.0 48.6 jit_solution(17500517937175614964)
XLA Ops:
  0.7 46.4 %galerkin.1 = f32[24,1344]{1,0:T(8,128)} custom-call(bf16[1,8,192,192]{3,2,1,0:T(8,128)(2,1)} %a_hbm.1, s32[1,8]{1,0:T(1,128)} %rows_hbm.1, s32[1,8]{1,0:T(1,128)} %cols_hbm.1, s32[1,1]{1,0:T(1,128)S(6)} %copy.8.count_hbm, bf16[2,2,192,192]{3,2,1,0:T(8,128)(2,1)} %p_hbm.1, s32[2,2048]{1,0:T(2,128)} %bitcast.1), custom_call_target="tpu_custom_call" | custom-call | tf_op jit(solution)/shard_map/galerkin/pallas_call | solution.py:444
  47.0 1.6 %copy.9 = f32[24,1344]{1,0:T(8,128)} copy(f32[24,1344]{1,0:T(8,128)} %galerkin.1) | data formatting | bytes 258048

commit v4 on v3

--- a/solution.py
+++ b/solution.py
@@ -19,10 +19,10 @@
 def kernel(
     a_hbm, rows_hbm, cols_hbm, count_hbm, p_hbm, pc_hbm, out_ref,
     a_buf, p_buf, rows_s, cols_s, count_s, pc_s,
-    own, halo0, halo1, halo2, relay, stack, left, side_left, prod,
+    own, halo0, halo1, halo2, stack, left, side_left, prod,
     mine, got0, got1, got2, side_mine, side_got0, side_got1, side_got2,
     part, lined0, lined1, lined2, side_part, side_lined0, side_lined1, side_lined2,
-    load_sem, halo_send, halo_recv, relay_send, relay_recv, skip_send,
+    load_sem, halo_send, halo_recv, skip_send,
     band_send, band_recv, side_send, side_recv, line_send, line_recv, side_line_send, side_line_recv,
 ):
     rows_n, cols_n = lax.axis_size("row"), lax.axis_size("col")
@@ -72,7 +72,7 @@
     for friend in friends:
         pl.semaphore_signal(barrier, inc=1, device_id=friend, device_id_type=MESH)
     expected = jnp.int32(len(friends))
-    for by in (1, -1, 2, -2, SPAN, -SPAN):
+    for by in (1, -1, 2, -2):
         expected += within(by).astype(jnp.int32)
 
         @pl.when(within(by))
@@ -100,6 +100,45 @@
                     empty_rows = jnp.zeros((share, size, LANES), halos[c].dtype)
                     halos[c][HB - far * share * by : HB - far * share * by + share] = empty_rows
 
+    for load in loads[2:]:
+        load.wait()
+    has = (r > 0, r < rows_n - 1)
+    edge = ((t < 2) & has[0]) | ((t >= cols_n - 2) & has[1])
+    outer = ((line_of == 0) & has[0]) | ((line_of == lines - 1) & has[1])
+    count = count_s[0, 0]
+    columns = [cols_s[0, s] for s in range(slots)]
+    picks = [jnp.clip(column - RB - t * share + HB, 0, halo0.shape[0] - 1) for column in columns]
+
+    def fill(centre):
+        for s in range(slots):
+            row = (r - 1) * RB + columns[s]
+            live = (count > s) & (row >= 0) & (row < rows_n * RB)
+            inside = (columns[s] >= RB) & (columns[s] < 2 * RB)
+            kept = live & (inside if centre else jnp.logical_not(inside))
+            line = jnp.clip(rows_s[0, s] - t * share, 0, share - 1)
+            for c in range(CHUNKS):
+                value = own[c, line]
+                stack[c, s * size : (s + 1) * size, :] = jnp.where(kept, value, jnp.zeros_like(value))
+
+    def turn(into):
+        flips = [stack[c].T for c in range(CHUNKS)]
+        into[0:LANES, :] = flips[0]
+        into[LANES:size, :] = flips[2][:half]
+        into[size : size + LANES, :] = flips[1]
+        into[size + LANES :, :] = flips[2][half:]
+
+    @pl.when(edge)
+    def _():
+        fill(False)
+        turn(side_left)
+
+    for k in range(2):
+
+        @pl.when(jnp.logical_not(has[k]))
+        def _():
+            for c in range(CHUNKS):
+                side_lined[c][k] = jnp.zeros((piece, LANES), jnp.float32)
+
     pl.semaphore_wait(barrier, expected)
 
     def halo_copy(source, target, device, sent, landed):
@@ -126,29 +165,15 @@
         source, target = rows_at(c, HB - share * by), rows_at(c, HB - 2 * share * by)
         return halo_copy(source, target, shifted(by), halo_send.at[c, 2 + n], halo_recv.at[c, 2 + n])
 
-    def to_relay(c, n):
-        by = 1 - 2 * n
-        across = r, t - (SPAN - 1) * by
-        source = rows_at(c, HB - share * by)
-        return halo_copy(source, relay.at[c], across, halo_send.at[c, 2 + n], relay_recv.at[c])
-
-    def from_relay(c, n):
+    def skip_copy(c, n):
         by = 1 - 2 * n
         target = rows_at(c, HB - 2 * share * by)
-        return halo_copy(relay.at[c], target, shifted(SPAN * by), relay_send.at[c], halo_recv.at[c, 2 + n])
-
-    def skip_copy(n):
-        by = 1 - 2 * n
-        c = CHUNKS - 1
-        target = rows_at(c, HB - 2 * share * by)
-        return halo_copy(own.at[c], target, shifted(2 * by), skip_send, halo_recv.at[c, 2 + n])
+        return halo_copy(own.at[c], target, shifted(2 * by), skip_send.at[c], halo_recv.at[c, 2 + n])
 
     turning, late, skips = (last, first), (first, last), (place == SPAN - 2, place == 1)
     ahead, behind = (within(1), within(-1)), (within(-1), within(1))
     skips = tuple(skips[n] & within(2 - 4 * n) for n in range(2))
-    relaying = tuple(late[n] & within(SPAN * (1 - 2 * n)) for n in range(2))
     far_on = tuple(jnp.logical_not(turning[n]) & behind[n] & ahead[n] for n in range(2))
-    relay_on = tuple(turning[n] & ahead[n] for n in range(2))
 
     def pass_fast(c):
         for n in range(2):
@@ -161,12 +186,6 @@
                 def _():
                     far_copy(c, n).start()
 
-                if c < CHUNKS - 1:
-
-                    @pl.when(relay_on[n])
-                    def _():
-                        to_relay(c, n).start()
-
     def pass_late(c):
         for n in range(2):
 
@@ -178,82 +197,30 @@
                 def _():
                     far_copy(c, n).start()
 
-    def pass_relay(c):
-        for n in range(2):
-
-            @pl.when(relaying[n])
-            def _():
-                to_relay(c, n).wait_recv()
-                from_relay(c, n).start()
+    def start_near(c, quick):
+        for n in range(2):
+
+            @pl.when(ahead[n] & (jnp.logical_not(turning[n]) if quick else turning[n]))
+            def _():
+                near_copy(c, n).start()
 
     for c in range(CHUNKS - 1):
-        for n in range(2):
-
-            @pl.when(ahead[n])
-            def _():
-                near_copy(c, n).start()
-
-    for n in range(2):
-
-        @pl.when(skips[n])
-        def _():
-            skip_copy(n).start()
-
-        @pl.when(jnp.logical_not(turning[n]) & ahead[n])
-        def _():
-            near_copy(CHUNKS - 1, n).start()
-
-    for load in loads[2:]:
-        load.wait()
-    edge = (t < 2) | (t >= cols_n - 2)
-    total_rows = rows_n * RB
-    count = count_s[0, 0]
-    picks = []
-    for s in range(slots):
-        column = cols_s[0, s]
-        row = (r - 1) * RB + column
-        live = (count > s) & (row >= 0) & (row < total_rows)
-        centre = (column >= RB) & (column < 2 * RB)
-        picks.append(jnp.clip(column - RB - t * share + HB, 0, halo0.shape[0] - 1))
-        line = jnp.clip(rows_s[0, s] - t * share, 0, share - 1)
-        for c in range(CHUNKS):
-            value = own[c, line]
-            zero = jnp.zeros_like(value)
-            stack[c, s * size : (s + 1) * size, :] = jnp.where(live & centre, value, zero)
-
-    def turn(into):
-        flips = [stack[c].T for c in range(CHUNKS)]
-        into[0:LANES, :] = flips[0]
-        into[LANES:size, :] = flips[2][:half]
-        into[size : size + LANES, :] = flips[1]
-        into[size + LANES :, :] = flips[2][half:]
-
+        start_near(c, True)
+        start_near(c, False)
+    for c in range(CHUNKS):
+        for n in range(2):
+
+            @pl.when(skips[n])
+            def _():
+                skip_copy(c, n).start()
+
+    start_near(CHUNKS - 1, True)
+    fill(True)
+    pass_fast(0)
     turn(left)
-    pass_fast(0)
     pass_fast(1)
-    for n in range(2):
-
-        @pl.when(relay_on[n])
-        def _():
-            near_copy(CHUNKS - 1, n).start()
-
-    pass_relay(0)
+    start_near(2, False)
     pass_fast(2)
-    pass_relay(1)
-
-    @pl.when(edge)
-    def _():
-        for s in range(slots):
-            column = cols_s[0, s]
-            row = (r - 1) * RB + column
-            live = (count > s) & (row >= 0) & (row < total_rows)
-            outside = (column < RB) | (column >= 2 * RB)
-            line = jnp.clip(rows_s[0, s] - t * share, 0, share - 1)
-            for c in range(CHUNKS):
-                value = own[c, line]
-                zero = jnp.zeros_like(value)
-                stack[c, s * size : (s + 1) * size, :] = jnp.where(live & outside, value, zero)
-        turn(side_left)
 
     def pieces(value):
         value = value.reshape(lines, SPAN, piece, LANES)
@@ -304,8 +271,6 @@
     def landed(ref, count, sem):
         some = ref.at[pl.ds(0, count)]
         pltpu.make_async_copy(some, some, sem).wait()
-
-    outer = (line_of == 0) | (line_of == lines - 1)
 
     def work(c):
         for n in range(2):
@@ -373,28 +338,16 @@
             def _():
                 far_copy(c, n).wait_send()
 
-            if c < CHUNKS - 1:
-
-                @pl.when(relay_on[n])
-                def _():
-                    to_relay(c, n).wait_send()
-
-                @pl.when(relaying[n])
-                def _():
-                    from_relay(c, n).wait_send()
-
-            else:
-
-                @pl.when(skips[n])
-                def _():
-                    skip_copy(n).wait_send()
+            @pl.when(skips[n])
+            def _():
+                skip_copy(c, n).wait_send()
 
     sums = []
     for c in range(CHUNKS):
         landed(lined[c], lines - 1, line_recv.at[c])
         for k in range(2):
 
-            @pl.when(line_of != k * (lines - 1))
+            @pl.when((line_of != k * (lines - 1)) & has[k])
             def _():
                 landed(side_lined[c], 1, side_line_recv.at[c, k])
 
@@ -455,7 +408,6 @@
             pltpu.SMEM((2, LANES), jnp.int32),
             pltpu.VMEM((CHUNKS, share, size, LANES), kind),
             halo, halo, halo,
-            pltpu.VMEM((CHUNKS, share, size, LANES), kind),
             pltpu.VMEM((CHUNKS, slots * size, LANES), kind),
             pltpu.VMEM((CR * size, slots * size), kind),
             pltpu.VMEM((CR * size, slots * size), kind),
@@ -472,8 +424,6 @@
             pltpu.SemaphoreType.DMA((CHUNKS, 4)),
             pltpu.SemaphoreType.DMA((CHUNKS, 4)),
             pltpu.SemaphoreType.DMA((CHUNKS,)),
-            pltpu.SemaphoreType.DMA((CHUNKS,)),
-            pltpu.SemaphoreType.DMA,
         ]
         + [pltpu.SemaphoreType.DMA((CHUNKS,))] * 7
         + [pltpu.SemaphoreType.DMA((CHUNKS, 2))],

time: 48.8 us -> 45.1 us (0.924); the launches traced: 48.6 us -> 44.3 us
  Pallas kernels: 46.4 us -> 42.1 us
    pallas_call x1, Pallas kernels: 46.4 us -> 42.1 us  [local(): pl.pallas_call(kernel, out_shape=jax.ShapeDtypeStruct((piece, 7 * size),...]
where the time goes in v4:
time: 45.1 us; the launch traced here: 44.3 us
  Pallas kernels  42.1 us (93%)
  local copies, waits for them, and re-layouts  1.57 us (3%)
  between operations  0.66 us (1%)
    pallas_call x1, Pallas kernels, local(): pl.pallas_call(kernel, out_shape=jax.ShapeDtypeStruct((piece, 7 * size),...  42.1 us
    unnamed x1, local copies, waits for them, and re-layouts  1.57 us

profile of v4, /device:TPU:960, one launch (start us, length us, event | category | flops | bytes accessed | tf_op | source)
XLA Modules:
  0.0 44.3 jit_solution(1885796369769427678)
XLA Ops:
  0.7 42.1 %galerkin.1 = f32[24,1344]{1,0:T(8,128)} custom-call(bf16[1,8,192,192]{3,2,1,0:T(8,128)(2,1)} %a_hbm.1, s32[1,8]{1,0:T(1,128)} %rows_hbm.1, s32[1,8]{1,0:T(1,128)} %cols_hbm.1, s32[1,1]{1,0:T(1,128)S(6)} %copy.8.count_hbm, bf16[2,2,192,192]{3,2,1,0:T(8,128)(2,1)} %p_hbm.1, s32[2,2048]{1,0:T(2,128)} %bitcast.1), custom_call_target="tpu_custom_call" | custom-call | tf_op jit(solution)/shard_map/galerkin/pallas_call | solution.py:397
  42.7 1.6 %copy.9 = f32[24,1344]{1,0:T(8,128)} copy(f32[24,1344]{1,0:T(8,128)} %galerkin.1) | data formatting | bytes 258048
